TPU v7x, 32 devices: a whole 2x2x4 slice. The times are simulated.
32 devices in a mesh: seq: 4 (over x, core), fsdp: 8 (over z, y).
Axes of the slice: x: 2, y: 2, z: 4, core: 2. Of those that a mesh axis runs over, the one named last changes fastest.
Arguments:
- queries: bfloat16 [8, 512, 3072], P('fsdp', 'seq'), may hold values from -6 to 6
- attn_keys: bfloat16 [8, 512, 3072], P('fsdp', 'seq'), may hold values from -6 to 6
- attn_values: bfloat16 [8, 512, 3072], P('fsdp', 'seq'), may hold values from -6 to 6
- grad_out: bfloat16 [8, 512, 6144], P('fsdp', 'seq'), may hold values from -6 to 6
- out_weight: bfloat16 [3072, 6144], P('seq', 'fsdp'), may hold values from -0.109375 to 0.109375
Outputs:
- grad_queries: bfloat16 [8, 512, 3072], P('fsdp', 'seq')
- grad_keys: bfloat16 [8, 512, 3072], P('fsdp', 'seq')
- grad_values: bfloat16 [8, 512, 3072], P('fsdp', 'seq')
- grad_weight: float32 [3072, 6144], P('seq', 'fsdp')
All inputs are finite; a program needn't handle non-finite values.
Results may differ from a plain program's by a relative error of at most 0.013.
Values may be sent and summed in bfloat16 or wider, within the bound.
A program may use at most 128 MiB of HBM per device.

v0:
```python
import jax
import jax.numpy as jnp
from jax import lax
from jax.sharding import PartitionSpec as P

HEAD_DIM = 128


def head_pass(q, k, v, dout):
    scale = 1.0 / q.shape[1] ** 0.5
    scores = jnp.dot(q, k.T, preferred_element_type=jnp.float32) * scale
    top = jnp.max(scores, axis=1, keepdims=True)
    expo = jnp.exp(scores - top)
    probs = expo / jnp.sum(expo, axis=1, keepdims=True)
    probs_low = probs.astype(jnp.bfloat16)
    attended = jnp.dot(probs_low, v, preferred_element_type=jnp.float32).astype(jnp.bfloat16)
    grad_v = jnp.dot(probs_low.T, dout, preferred_element_type=jnp.float32).astype(jnp.bfloat16)
    grad_probs = jnp.dot(dout, v.T, preferred_element_type=jnp.float32)
    delta = jnp.sum(dout.astype(jnp.float32) * attended.astype(jnp.float32), axis=1, keepdims=True)
    grad_scores = (probs * (grad_probs - delta)).astype(jnp.bfloat16)
    grad_q = (jnp.dot(grad_scores, k, preferred_element_type=jnp.float32) * scale).astype(
        jnp.bfloat16
    )
    grad_k = (jnp.dot(grad_scores.T, q, preferred_element_type=jnp.float32) * scale).astype(
        jnp.bfloat16
    )
    return (attended, grad_q, grad_k, grad_v)


def shards(queries, attn_keys, attn_values, grad_out, out_weight):
    groups = lax.axis_size("seq")
    local_width = queries.shape[2] // groups
    heads_here = local_width // HEAD_DIM
    head_q, head_k, head_v = (
        lax.all_to_all(queries, "seq", split_axis=2, concat_axis=1, tiled=True),
        lax.all_to_all(attn_keys, "seq", split_axis=2, concat_axis=1, tiled=True),
        lax.all_to_all(attn_values, "seq", split_axis=2, concat_axis=1, tiled=True),
    )
    every_rows = lax.all_gather(grad_out, "seq", axis=1, tiled=True)
    flat_rows = every_rows.reshape(-1, every_rows.shape[2])
    dout = lax.dot_general(
        flat_rows,
        lax.all_gather(out_weight, "fsdp", axis=1, tiled=True),
        (((1,), (1,)), ((), ())),
        preferred_element_type=jnp.float32,
    ).astype(jnp.bfloat16)
    head_q = head_q[0]
    head_k = head_k[0]
    head_v = head_v[0]
    pieces = []
    for index in range(heads_here):
        lower = index * HEAD_DIM
        result = head_pass(
            head_q[:, lower : lower + HEAD_DIM],
            head_k[:, lower : lower + HEAD_DIM],
            head_v[:, lower : lower + HEAD_DIM],
            dout[:, lower : lower + HEAD_DIM],
        )
        pieces.append(result)
    attended = jnp.concatenate([item[0] for item in pieces], axis=1)
    grad_q, grad_k, grad_v = (
        lax.all_to_all(
            jnp.concatenate([item[1] for item in pieces], axis=1)[None],
            "seq",
            split_axis=1,
            concat_axis=2,
            tiled=True,
        ),
        lax.all_to_all(
            jnp.concatenate([item[2] for item in pieces], axis=1)[None],
            "seq",
            split_axis=1,
            concat_axis=2,
            tiled=True,
        ),
        lax.all_to_all(
            jnp.concatenate([item[3] for item in pieces], axis=1)[None],
            "seq",
            split_axis=1,
            concat_axis=2,
            tiled=True,
        ),
    )
    whole = lax.dot_general(
        attended, flat_rows, (((0,), (0,)), ((), ())), preferred_element_type=jnp.float32
    )
    grad_weight = lax.psum_scatter(whole, "fsdp", scatter_dimension=1, tiled=True)
    return (grad_q, grad_k, grad_v, grad_weight)


def solution(mesh):
    return jax.shard_map(
        shards,
        mesh=mesh,
        in_specs=(
            P("fsdp", "seq", None),
            P("fsdp", "seq", None),
            P("fsdp", "seq", None),
            P("fsdp", "seq", None),
            P("seq", "fsdp"),
        ),
        out_specs=(
            P("fsdp", "seq", None),
            P("fsdp", "seq", None),
            P("fsdp", "seq", None),
            P("seq", "fsdp"),
        ),
        check_vma=False,
    )
```

profile of v0, /device:TPU:0, one launch (start us, length us, event | category | flops | bytes accessed | tf_op | source)
XLA Modules:
  0.0 552.7 jit_solution(6435645390018766886)
XLA Ops:
  8.7 1.9 copy.105
  11.1 16.9 %reduce.1 = bf16[3072,128]{1,0:T(8,128)(2,1)S(1)} reduce(bf16[3072,1,128]{2,1,0:T(2,128)(2,1)S(1)} %bitcast.82, bf16[]{:T(256)} %broadcast.44), dimensions={1}, to_apply=%bitcast.36.reduce_sub_computation | reduce | bytes 1572866
  27.9 1.0 reshape.35
  28.9 4.3 all-to-all-start
  33.3 1.9 copy.107
  35.1 16.9 %reduce = bf16[3072,128]{1,0:T(8,128)(2,1)S(1)} reduce(bf16[3072,1,128]{2,1,0:T(2,128)(2,1)S(1)} %bitcast.92, bf16[]{:T(256)} %broadcast.44), dimensions={1}, to_apply=%bitcast.34.reduce_sub_computation | reduce | bytes 1572866
  52.0 1.0 reshape.33
  53.8 4.7 all-to-all-start.1
  58.5 1.9 copy.109
  60.4 16.9 %reduce.2 = bf16[3072,128]{1,0:T(8,128)(2,1)S(1)} reduce(bf16[3072,1,128]{2,1,0:T(2,128)(2,1)S(1)} %bitcast.93, bf16[]{:T(256)} %broadcast.44), dimensions={1}, to_apply=%bitcast.38.reduce_sub_computation | reduce | bytes 1572866
  77.3 1.0 reshape.37
  78.2 3.5 all-to-all-start.2
  82.7 1.2 copy.106
  83.9 2.4 reshape.34
  86.4 1.2 copy.108
  87.6 5.8 %all-to-all-done.2 = bf16[4,2,49152]{2,1,0:T(2,128)(2,1)S(1)} async-done(((bf16[4,2,49152]{2,1,0:T(2,128)(2,1)}), bf16[4,2,49152]{2,1,0:T(2,128)(2,1)S(1)}, u32[]{:S(2)}, u32[]{:S(2)}) %all-to-all-start.2) | async-done | bytes 786464 | tf_op jit(solution)/shard_map/all_to_all | solution.py:37
  94.3 1.2 copy.110
  95.4 1.3 fusion.115
  96.8 1.0 fusion.60
  97.7 1.3 fusion.120
  99.2 1.3 fusion.119
  100.7 1.3 fusion.118
  102.2 1.3 fusion.117
  103.7 1.5 fusion.116
  105.7 1.2 copy-done.18
  106.9 1.0 constant_dynamic-update-slice_fusion.5
  108.1 1.0 constant_dynamic-update-slice_fusion.4
  109.3 1.0 constant_dynamic-update-slice_fusion.3
  110.5 1.1 constant_dynamic-update-slice_fusion.2
  112.6 1.0 constant_dynamic-update-slice_fusion.1
  113.7 96.7 %all-gather.5.cloned.1.call-done = bf16[768,6144]{1,0:T(8,128)(2,1)} async-done(((bf16[768,768]{1,0:T(8,128)(2,1)}), bf16[768,6144]{1,0:T(8,128)(2,1)}) %all-gather.5.cloned.1.call-update) | async-done | bytes 9437200 | tf_op jit(solution)/shard_map/all_gather | solution.py:43
  210.3 10.1 %fusion.4 = bf16[512,768]{1,0:T(8,128)(2,1)S(1)} fusion(bf16[768,6144]{1,0:T(8,128)(2,1)} %all-gather.5.cloned.1.call-done, bf16[1,512,6144]{2,1,0:T(8,128)(2,1)} %all-gather.3.cloned.1.call-done), kind=kOutput, calls=%fused_computation.4 | convolution fusion | flops 4832231424 | bytes 16515072 | tf_op jit(solution)/shard_map/dot_general | solution.py:41
  220.5 2.5 multiply_reduce_fusion
  223.6 10.5 %fusion = f32[768,6144]{1,0:T(8,128)} fusion(bf16[512,768]{1,0:T(8,128)(2,1)} %constant_dynamic-update-slice_fusion, bf16[1,512,6144]{2,1,0:T(8,128)(2,1)S(1)} %copy-done.4), kind=kOutput, calls=%fused_computation | convolution fusion | flops 4831838208 | bytes 25952256 | tf_op jit(solution)/shard_map/dot_general | solution.py:84
  234.2 1.5 fusion.48
  235.7 1.5 fusion.47
  237.2 1.2 fusion.46
  239.5 1.0 copy-done.21
  240.4 4.8 copy.127
  245.2 7.3 %reduce.5 = bf16[512,768]{1,0:T(8,128)(2,1)} reduce(bf16[512,1,768]{2,1,0:T(2,128)(2,1)} %bitcast.87, bf16[]{:T(256)} %broadcast.44), dimensions={1}, to_apply=%bitcast.44.reduce_sub_computation | reduce | bytes 1572866
  252.5 2.0 reshape.43
  254.5 4.4 all-to-all-start.5
  259.0 1.9 fusion.18
  260.9 2.0 fusion.32
  269.6 3.7 copy.123
  273.3 5.4 reduce.3
  278.7 1.0 reshape.39
  280.2 1.4 fusion.34
  281.6 1.4 fusion.36
  283.0 3.8 all-to-all-start.3
  287.1 1.3 fusion.40
  288.4 1.3 fusion.42
  289.8 1.6 copy.125
  291.4 5.3 reduce.4
  296.7 1.0 reshape.41
  298.4 3.5 all-to-all-start.4
  301.9 2.4 reshape.44
  304.3 1.0 copy.149
  305.3 1.5 copy.128
  306.8 1.2 copy.131
  309.2 1.2 copy.129
  310.4 3.1 all-to-all-done.4
  314.7 1.2 copy.130
  315.9 229.8 %reduce-scatter.2.cloned.1.call-done = f32[768,768]{1,0:T(8,128)} async-done(((f32[768,6144]{1,0:T(8,128)}), f32[768,768]{1,0:T(8,128)}) %reduce-scatter.2.cloned.1.call-update) | async-done | bytes 2359312 | tf_op jit(solution)/shard_map/reduce_scatter | solution.py:87
  (163 shorter events, 19.6 us)
Async XLA Ops:
  7.2 1.5 copy-start.22
  7.2 106.5 %all-gather.3.cloned.1.call-start = ((), (), s32[]{:S(2)}) async-start(), calls=%async_computation.7 | async-start | bytes 7864320 | tf_op jit(solution)/shard_map/all_gather | solution.py:39
  7.9 202.4 %all-gather.5.cloned.1.call-start = ((), (), s32[]{:S(2)}) async-start(), calls=%async_computation.8 | async-start | bytes 10616832 | tf_op jit(solution)/shard_map/all_gather | solution.py:43
  28.9 4.3 copy-start.23
  28.9 24.9 %all-to-all-start = ((bf16[4,2,49152]{2,1,0:T(2,128)(2,1)}), bf16[4,2,49152]{2,1,0:T(2,128)(2,1)S(1)}, u32[]{:S(2)}, u32[]{:S(2)}) async-start(bf16[4,2,49152]{2,1,0:T(2,128)(2,1)} %reshape.35), calls=%async_computation | async-start | bytes 1572864 | tf_op jit(solution)/shard_map/all_to_all | solution.py:35
  53.0 5.5 copy-start.24
  53.8 24.5 %all-to-all-start.1 = ((bf16[4,2,49152]{2,1,0:T(2,128)(2,1)}), bf16[4,2,49152]{2,1,0:T(2,128)(2,1)}, u32[]{:S(2)}, u32[]{:S(2)}) async-start(bf16[4,2,49152]{2,1,0:T(2,128)(2,1)} %reshape.33), calls=%async_computation.1 | async-start | bytes 1572864 | tf_op jit(solution)/shard_map/all_to_all | solution.py:36
  78.2 15.2 %all-to-all-start.2 = ((bf16[4,2,49152]{2,1,0:T(2,128)(2,1)}), bf16[4,2,49152]{2,1,0:T(2,128)(2,1)S(1)}, u32[]{:S(2)}, u32[]{:S(2)}) async-start(bf16[4,2,49152]{2,1,0:T(2,128)(2,1)} %reshape.37), calls=%async_computation.2 | async-start | bytes 1572864 | tf_op jit(solution)/shard_map/all_to_all | solution.py:37
  81.8 463.9 %reduce-scatter.2.cloned.1.call-start = ((), (), s32[]{:S(2)}) async-start(), calls=%async_computation.9 | async-start | bytes 21233664 | tf_op jit(solution)/shard_map/reduce_scatter | solution.py:87
  96.7 2.5 copy-start.13
  96.7 2.5 copy-start.39
  99.2 12.4 %copy-start.41 = (f32[512]{0:T(512)}, f32[512]{0:T(512)S(1)}, u32[]{:S(2)}) copy-start(f32[512]{0:T(512)S(1)} %fusion.58) | copy-start | bytes 6148
  100.7 9.6 %copy-start.43 = (f32[512]{0:T(512)}, f32[512]{0:T(512)S(1)}, u32[]{:S(2)}) copy-start(f32[512]{0:T(512)S(1)} %fusion.56) | copy-start | bytes 6148
  102.2 6.9 %copy-start.45 = (f32[512]{0:T(512)}, f32[512]{0:T(512)S(1)}, u32[]{:S(2)}) copy-start(f32[512]{0:T(512)S(1)} %fusion.54) | copy-start | bytes 6148
  103.5 4.4 copy-start
  103.7 4.2 copy-start.47
  105.2 2.7 copy-start.2
  105.2 1.7 copy-start.18
  105.4 2.7 copy-start.49
  105.7 3.4 copy-start.5
  108.1 2.2 copy-start.6
  109.3 2.3 copy-start.7
  110.5 1.3 copy-start.9
  111.8 0.8 copy-start.11
  210.3 10.1 %copy-start.14 = (f32[512,512]{0,1:T(8,128)S(1)}, f32[512,512]{0,1:T(8,128)}, u32[]{:S(2)}) copy-start(f32[512,512]{0,1:T(8,128)} %copy-done.13) | copy-start | bytes 3145732
  210.3 10.1 %copy-start.35 = (bf16[512,128]{1,0:T(8,128)(2,1)S(1)}, bf16[512,128]{1,0:T(8,128)(2,1)}, u32[]{:S(2)}) copy-start(bf16[512,128]{1,0:T(8,128)(2,1)} %get-tuple-element.34) | copy-start | bytes 393220
  210.3 10.1 %copy-start.36 = (bf16[512,128]{1,0:T(8,128)(2,1)S(1)}, bf16[512,128]{1,0:T(8,128)(2,1)}, u32[]{:S(2)}) copy-start(bf16[512,128]{1,0:T(8,128)(2,1)} %get-tuple-element.36) | copy-start | bytes 393220
  210.3 13.3 %copy-start.4 = (bf16[1,512,6144]{2,1,0:T(8,128)(2,1)S(1)}, bf16[1,512,6144]{2,1,0:T(8,128)(2,1)}, u32[]{:S(2)}) copy-start(bf16[1,512,6144]{2,1,0:T(8,128)(2,1)} %all-gather.3.cloned.1.call-done) | copy-start | bytes 18874372
  220.4 2.5 copy-start.26
  234.1 3.1 copy-start.8
  234.1 4.3 copy-start.10
  234.1 4.3 copy-start.27
  234.1 4.6 copy-start.12
  235.7 3.4 copy-start.15
  235.7 3.4 copy-start.40
  235.7 3.4 copy-start.51
  239.5 1.0 copy-start.21
  252.5 6.4 %copy-start.38 = (f32[512]{0:T(512)S(1)}, f32[512]{0:T(512)}, u32[]{:S(2)}) copy-start(f32[512]{0:T(512)} %copy-done.37) | copy-start | bytes 6148
  252.5 6.4 %copy-start.50 = (f32[512]{0:T(512)S(1)}, f32[512]{0:T(512)}, u32[]{:S(2)}) copy-start(f32[512]{0:T(512)} %copy-done.49) | copy-start | bytes 6148
  252.5 6.4 %copy-start.57 = (f32[512]{0:T(512)S(1)}, f32[512]{0:T(512)}, u32[]{:S(2)}) copy-start(f32[512]{0:T(512)} %get-tuple-element.9) | copy-start | bytes 6148
  254.5 28.5 %all-to-all-start.5 = ((bf16[4,2,49152]{2,1,0:T(2,128)(2,1)}), bf16[4,2,49152]{2,1,0:T(2,128)(2,1)}, u32[]{:S(2)}, u32[]{:S(2)}) async-start(bf16[4,2,49152]{2,1,0:T(2,128)(2,1)} %reshape.43), calls=%async_computation.5 | async-start | bytes 1572864 | tf_op jit(solution)/shard_map/all_to_all | solution.py:76
  258.9 3.9 copy-start.17
  258.9 4.2 copy-start.19
  258.9 4.2 copy-start.28
  260.8 2.3 copy-start.1
  260.9 2.3 copy-start.48
  260.9 2.3 copy-start.56
  263.5 0.8 copy-start.31
  263.9 1.3 copy-start.44
  263.9 1.3 copy-start.54
  264.3 0.8 copy-start.33
  265.1 1.2 copy-start.42
  265.1 1.2 copy-start.53
  265.4 0.8 copy-start.29
  266.3 1.2 copy-start.16
  266.3 1.2 copy-start.52
  266.6 1.2 copy-start.32
  267.9 0.8 copy-start.34
  268.7 0.9 copy-start.25
  273.3 6.4 %copy-start.3 = (bf16[1,4,128,768]{3,2,1,0:T(8,128)(2,1)S(1)}, bf16[1,4,128,768]{3,2,1,0:T(8,128)(2,1)}, u32[]{:S(2)}) copy-start(bf16[1,4,128,768]{3,2,1,0:T(8,128)(2,1)} %copy.106) | copy-start | bytes 2359300
  278.7 1.5 copy-start.20
  280.2 6.6 %copy-start.30 = (bf16[512,512]{0,1:T(8,128)(2,1)S(1)}, bf16[512,512]{0,1:T(8,128)(2,1)}, u32[]{:S(2)}) copy-start(bf16[512,512]{0,1:T(8,128)(2,1)} %copy-done.29) | copy-start | bytes 1572868
  283.0 15.4 %all-to-all-start.3 = ((bf16[4,2,49152]{2,1,0:T(2,128)(2,1)}), bf16[4,2,49152]{2,1,0:T(2,128)(2,1)S(1)}, u32[]{:S(2)}, u32[]{:S(2)}) async-start(bf16[4,2,49152]{2,1,0:T(2,128)(2,1)} %reshape.39), calls=%async_computation.3 | async-start | bytes 1572864 | tf_op jit(solution)/shard_map/all_to_all | solution.py:62
  298.4 15.1 %all-to-all-start.4 = ((bf16[4,2,49152]{2,1,0:T(2,128)(2,1)}), bf16[4,2,49152]{2,1,0:T(2,128)(2,1)S(1)}, u32[]{:S(2)}, u32[]{:S(2)}) async-start(bf16[4,2,49152]{2,1,0:T(2,128)(2,1)} %reshape.41), calls=%async_computation.4 | async-start | bytes 1572864 | tf_op jit(solution)/shard_map/all_to_all | solution.py:69
  (3 other events, 1.9 us)
Sparse Core Ops, SparseCore 0:
  9.6 61.3 all-gather.2
  73.1 137.1 all-gather.4
  234.2 311.4 reduce-scatter.1
where the time goes:
time: 562 us; the launch traced here: 553 us
  waiting for transfers between devices  338 us (60%)
  other arithmetic  71.4 us (13%)
  matrix products  54 us (10%)
  local copies, waits for them, and re-layouts  49.6 us (9%)
  starting transfers between devices  24.3 us (4%)
  between operations  15.2 us (3%)
    reduce_scatter x1, waiting for transfers between devices, shards(): lax.psum_scatter(whole, 'fsdp', scatter_dimension=1, tiled=True)  230 us
    all_gather x1, waiting for transfers between devices, shards(): lax.all_gather(out_weight, 'fsdp', axis=1, tiled=True)  96.7 us
    unnamed x6, other arithmetic  68.6 us
    unnamed x141, local copies, waits for them, and re-layouts  33 us
  transfers between devices with their start and end apart: 9, of which 6 were waited for; matrix products, arithmetic and copies ran while one was open for 26% of the time, Pallas kernels for 0%

commit v1 on v0

v1 whole, which is shorter than its diff:
```python
import jax
import jax.numpy as jnp
from jax import lax
from jax.experimental import pallas as pl
from jax.experimental.pallas import tpu as pltpu
from jax.sharding import PartitionSpec as P

HEAD_DIM = 128
TILE = 256
MESH = pl.DeviceIdType.MESH
F32, BF16 = jnp.float32, jnp.bfloat16
NT = (((1,), (1,)), ((), ()))
TN = (((0,), (0,)), ((), ()))


def kernel(
    q_ref, k_ref, v_ref, go_ref, w_ref,
    gq_out, gk_out, gv_out, gw_out,
    qkv, g, w, att, probs, keep, psend, pgot, zsend, zgot, dout, grads, gwsend, gwgot,
    send, recv, local,
):
    s, f = lax.axis_index("seq"), lax.axis_index("fsdp")
    tokens = q_ref.shape[1]
    width = w_ref.shape[0]
    block = w_ref.shape[1]
    heads = width // HEAD_DIM
    scale = 1.0 / HEAD_DIM**0.5
    core = s + 1 - 2 * (s % 2)
    across = s + 2 - 4 * (s // 2)
    both = core + 2 - 4 * (core // 2)
    f_y = f + 1 - 2 * (f % 2)
    f_z = f + 2 - 4 * ((f // 2) % 2)
    f_yz = f_z + 1 - 2 * (f_z % 2)

    def other_half(i):
        return i + 4 - 8 * (i // 4)

    tok_peer = [None] + [{"seq": i, "fsdp": f} for i in (core, across, both)]
    tok_id = [s, core, across, both]
    row_peer = [None] + [{"seq": s, "fsdp": i} for i in (f_y, f_z, f_yz)]
    row_id = [f, f_y, f_z, f_yz]
    far = {"seq": s, "fsdp": other_half(f)}

    barrier = pltpu.get_barrier_semaphore()
    peers = tok_peer[1:] + row_peer[1:] + [far]
    for peer in peers:
        pl.semaphore_signal(barrier, inc=1, device_id=peer, device_id_type=MESH)
    pl.semaphore_wait(barrier, len(peers))

    count = [0, 0]
    pending = []

    def push(src, dst, peer):
        i = count[0]
        count[0] += 1
        copy = pltpu.make_async_remote_copy(
            src_ref=src, dst_ref=dst, send_sem=send.at[i], recv_sem=recv.at[i],
            device_id=peer, device_id_type=MESH,
        )
        copy.start()
        pending.append(copy)
        return copy

    def here(src, dst):
        i = count[1]
        count[1] += 1
        copy = pltpu.make_async_copy(src, dst, local.at[i])
        copy.start()
        return copy

    def cols(i, size):
        return pl.ds(pl.multiple_of(i * size, 128), size)

    def rows(t):
        return pl.ds(t * tokens, tokens)

    own = []
    for c in range(2):
        owner = f if c == 0 else other_half(f)
        own.append(here(go_ref.at[0, :, cols(owner, block)], g.at[0, rows(0), pl.ds(c * block, block)]))
    got_g = {}
    for r in (3, 1, 2):
        for c in range(2):
            owner = row_id[r] if c == 0 else other_half(row_id[r])
            got_g[r, c] = push(
                go_ref.at[0, :, cols(owner, block)], g.at[r, rows(0), pl.ds(c * block, block)], row_peer[r]
            )
    got_w = push(w_ref, w.at[:, pl.ds(block, block)], far)
    own_w = here(w_ref, w.at[:, pl.ds(0, block)])
    got_qkv, own_qkv = [], []
    for a, ref in enumerate((q_ref, k_ref, v_ref)):
        for t in (2, 3, 1):
            got_qkv.append(push(ref.at[0, :, cols(tok_id[t], width)], qkv.at[a, rows(t)], tok_peer[t]))
        own_qkv.append(here(ref.at[0, :, cols(s, width)], qkv.at[a, rows(0)]))

    got_g2 = {}

    def spread(r):
        for t in (2, 1):
            got_g2[r, t] = push(g.at[r, rows(0)], g.at[r, rows(t)], tok_peer[t])

    for copy in own:
        copy.wait()
    spread(0)
    for r in (1, 2, 3):
        got_g[r, 0].wait_recv()
        got_g[r, 1].wait_recv()
        spread(r)

    for copy in own_qkv:
        copy.wait()
    for copy in got_qkv:
        copy.wait_recv()

    def forward(h, carry):
        hc = cols(h, HEAD_DIM)
        scores = lax.dot_general(qkv[0, :, hc], qkv[1, :, hc], NT, preferred_element_type=F32) * scale
        expo = jnp.exp(scores - jnp.max(scores, axis=1, keepdims=True))
        p = expo / jnp.sum(expo, axis=1, keepdims=True)
        probs[h] = p
        att[0, :, hc] = jnp.dot(p.astype(BF16), qkv[2, :, hc], preferred_element_type=F32).astype(BF16)
        return carry

    chunks = width // TILE
    per = TILE // HEAD_DIM
    got_att = {}
    for c in range(chunks):
        lax.fori_loop(c * per, (c + 1) * per, forward, 0)
        cc = pl.ds(c * TILE, TILE)
        got_att[1, c] = push(att.at[0, :, cc], att.at[1, :, cc], row_peer[1])
        got_att[2, c] = push(att.at[0, :, cc], att.at[2, :, cc], row_peer[2])

    for r in range(4):
        got_g2[r, 2].wait_recv()
        got_g2[r, 3] = push(g.at[r, rows(2)], g.at[r, rows(3)], tok_peer[1])
    own_w.wait()
    got_w.wait_recv()

    def partial(r, c):
        return lax.dot_general(g[r], w[pl.ds(c * TILE, TILE), :], NT, preferred_element_type=F32)

    def whole_rows(r):
        got_g2[r, 1].wait_recv()
        got_g2[r, 3].wait_recv()

    got_p = {}
    whole_rows(3)
    whole_rows(1)
    for c in range(chunks):
        cc = pl.ds(c * TILE, TILE)
        for slot, r in ((1, 3), (0, 1)):
            psend[slot, :, cc] = partial(r, c).astype(BF16)
            got_p[slot, c] = push(psend.at[slot, :, cc], pgot.at[slot, :, cc], row_peer[1])
    whole_rows(2)
    whole_rows(0)
    for c in range(chunks):
        cc = pl.ds(c * TILE, TILE)
        keep[1, :, cc] = partial(2, c)
        keep[0, :, cc] = partial(0, c)
        got_att[2, c].wait_recv()
        got_att[3, c] = push(att.at[2, :, cc], att.at[3, :, cc], row_peer[1])

    for c in range(chunks):
        got_att[1, c].wait_recv()
        got_att[3, c].wait_recv()

    def weight_tile(start):
        total = jnp.zeros((width, TILE), F32)
        for r in range(4):
            total += lax.dot_general(att[r], g[r, :, pl.ds(start, TILE)], TN, preferred_element_type=F32)
        return total

    got_gw = []
    for c in range(block // TILE):
        cc = pl.ds(c * TILE, TILE)
        gwsend[:, cc] = weight_tile(block + c * TILE).astype(BF16)
        got_gw.append(push(gwsend.at[:, cc], gwgot.at[:, cc], far))

    got_z = []
    for c in range(chunks):
        cc = pl.ds(c * TILE, TILE)
        got_p[1, c].wait_recv()
        zsend[:, cc] = (keep[1, :, cc] + pgot[1, :, cc].astype(F32)).astype(BF16)
        got_z.append(push(zsend.at[:, cc], zgot.at[:, cc], row_peer[2]))

    for c in range(block // TILE):
        gw_out[:, pl.ds(c * TILE, TILE)] = weight_tile(c * TILE)

    outs = (gq_out, gk_out, gv_out)
    base = count[0]
    count[0] += 9

    def home(a, t, hc, start, size):
        i = base + a * 3 + t - 1
        return pltpu.make_async_remote_copy(
            src_ref=grads.at[a, rows(t), hc],
            dst_ref=outs[a].at[0, :, pl.ds(pl.multiple_of(start, 128), size)],
            send_sem=send.at[i], recv_sem=recv.at[i],
            device_id=tok_peer[t], device_id_type=MESH,
        )

    def backward(h, carry):
        hc = cols(h, HEAD_DIM)
        q, k, v, do = qkv[0, :, hc], qkv[1, :, hc], qkv[2, :, hc], dout[:, hc]
        p = probs[h]
        delta = jnp.sum(do.astype(F32) * att[0, :, hc].astype(F32), axis=1, keepdims=True)
        grad_p = lax.dot_general(do, v, NT, preferred_element_type=F32)
        grad_s = (p * (grad_p - delta)).astype(BF16)
        grads[0, :, hc] = (jnp.dot(grad_s, k, preferred_element_type=F32) * scale).astype(BF16)
        grads[1, :, hc] = (lax.dot_general(grad_s, q, TN, preferred_element_type=F32) * scale).astype(BF16)
        grads[2, :, hc] = lax.dot_general(p.astype(BF16), do, TN, preferred_element_type=F32).astype(BF16)
        for a in range(3):
            for t in (2, 3, 1):
                home(a, t, hc, s * width + h * HEAD_DIM, HEAD_DIM).start()
        return carry

    for c in range(chunks):
        cc = pl.ds(c * TILE, TILE)
        got_p[0, c].wait_recv()
        got_z[c].wait_recv()
        dout[:, cc] = (keep[0, :, cc] + pgot[0, :, cc].astype(F32) + zgot[:, cc].astype(F32)).astype(BF16)
        lax.fori_loop(c * per, (c + 1) * per, backward, 0)

    last = [here(grads.at[a, rows(0)], outs[a].at[0, :, cols(s, width)]) for a in range(3)]
    for copy in got_gw:
        copy.wait_recv()
    gw_out[...] += gwgot[...].astype(F32)
    for a in range(3):
        for t in (1, 2, 3):
            whole = home(a, t, pl.ds(0, width), s * width, width)
            whole.wait_send()
            whole.wait_recv()
    for copy in last:
        copy.wait()
    for copy in pending:
        copy.wait_send()


def fused(queries, attn_keys, attn_values, grad_out, out_weight):
    tokens = queries.shape[1]
    length = tokens * lax.axis_size("seq")
    width, block = out_weight.shape
    heads = width // HEAD_DIM
    any_spec = pl.BlockSpec(memory_space=pl.ANY)
    flops = 4 * length * width * grad_out.shape[2] + 12 * heads * length * length * HEAD_DIM
    return pl.pallas_call(
        kernel,
        out_shape=(
            jax.ShapeDtypeStruct(queries.shape, BF16),
            jax.ShapeDtypeStruct(queries.shape, BF16),
            jax.ShapeDtypeStruct(queries.shape, BF16),
            jax.ShapeDtypeStruct(out_weight.shape, F32),
        ),
        in_specs=[any_spec] * 5,
        out_specs=(any_spec, any_spec, any_spec, pl.BlockSpec(memory_space=pltpu.VMEM)),
        scratch_shapes=[
            pltpu.VMEM((3, length, width), BF16),
            pltpu.VMEM((4, length, 2 * block), BF16),
            pltpu.VMEM((width, 2 * block), BF16),
            pltpu.VMEM((4, length, width), BF16),
            pltpu.VMEM((heads, length, length), F32),
            pltpu.VMEM((2, length, width), F32),
            pltpu.VMEM((2, length, width), BF16),
            pltpu.VMEM((2, length, width), BF16),
            pltpu.VMEM((length, width), BF16),
            pltpu.VMEM((length, width), BF16),
            pltpu.VMEM((length, width), BF16),
            pltpu.VMEM((3, length, width), BF16),
            pltpu.VMEM((width, block), BF16),
            pltpu.VMEM((width, block), BF16),
            pltpu.SemaphoreType.DMA((72,)),
            pltpu.SemaphoreType.DMA((72,)),
            pltpu.SemaphoreType.DMA((16,)),
        ],
        compiler_params=pltpu.CompilerParams(
            collective_id=0, has_side_effects=True, vmem_limit_bytes=60 * 1024 * 1024
        ),
        cost_estimate=pl.CostEstimate(flops=flops, bytes_accessed=20 * 1024 * 1024, transcendentals=0),
    )(queries, attn_keys, attn_values, grad_out, out_weight)


def head_pass(q, k, v, dout):
    scale = 1.0 / q.shape[1] ** 0.5
    scores = jnp.dot(q, k.T, preferred_element_type=F32) * scale
    expo = jnp.exp(scores - jnp.max(scores, axis=1, keepdims=True))
    probs = expo / jnp.sum(expo, axis=1, keepdims=True)
    probs_low = probs.astype(BF16)
    attended = jnp.dot(probs_low, v, preferred_element_type=F32).astype(BF16)
    grad_v = jnp.dot(probs_low.T, dout, preferred_element_type=F32).astype(BF16)
    grad_probs = jnp.dot(dout, v.T, preferred_element_type=F32)
    delta = jnp.sum(dout.astype(F32) * attended.astype(F32), axis=1, keepdims=True)
    grad_scores = (probs * (grad_probs - delta)).astype(BF16)
    grad_q = (jnp.dot(grad_scores, k, preferred_element_type=F32) * scale).astype(BF16)
    grad_k = (jnp.dot(grad_scores.T, q, preferred_element_type=F32) * scale).astype(BF16)
    return attended, grad_q, grad_k, grad_v


def collectives(queries, attn_keys, attn_values, grad_out, out_weight):
    width = queries.shape[2] // lax.axis_size("seq")
    q, k, v = (
        lax.all_to_all(x, "seq", split_axis=2, concat_axis=1, tiled=True)[0]
        for x in (queries, attn_keys, attn_values)
    )
    every_rows = lax.all_gather(grad_out, "seq", axis=1, tiled=True)
    flat_rows = every_rows.reshape(-1, every_rows.shape[2])
    weight = lax.all_gather(out_weight, "fsdp", axis=1, tiled=True)
    dout = lax.dot_general(flat_rows, weight, NT, preferred_element_type=F32).astype(BF16)
    pieces = []
    for lower in range(0, width, HEAD_DIM):
        here = slice(lower, lower + HEAD_DIM)
        pieces.append(head_pass(q[:, here], k[:, here], v[:, here], dout[:, here]))
    attended = jnp.concatenate([item[0] for item in pieces], axis=1)
    grads = [
        lax.all_to_all(
            jnp.concatenate([item[i] for item in pieces], axis=1)[None],
            "seq", split_axis=1, concat_axis=2, tiled=True,
        )
        for i in (1, 2, 3)
    ]
    whole = lax.dot_general(attended, flat_rows, TN, preferred_element_type=F32)
    return (*grads, lax.psum_scatter(whole, "fsdp", scatter_dimension=1, tiled=True))


def shards(queries, attn_keys, attn_values, grad_out, out_weight):
    width, block = out_weight.shape
    fits = lax.axis_size("seq") == 4 and lax.axis_size("fsdp") == 8
    if fits and queries.shape[0] == 1 and queries.shape[1] % 16 == 0 and width % TILE == 0 and block % TILE == 0:
        return fused(queries, attn_keys, attn_values, grad_out, out_weight)
    return collectives(queries, attn_keys, attn_values, grad_out, out_weight)


def solution(mesh):
    return jax.shard_map(
        shards,
        mesh=mesh,
        in_specs=(
            P("fsdp", "seq", None),
            P("fsdp", "seq", None),
            P("fsdp", "seq", None),
            P("fsdp", "seq", None),
            P("seq", "fsdp"),
        ),
        out_specs=(
            P("fsdp", "seq", None),
            P("fsdp", "seq", None),
            P("fsdp", "seq", None),
            P("seq", "fsdp"),
        ),
        check_vma=False,
    )
```

time: 562 us -> 191 us (0.34)
  the two profiles are of different devices: /device:TPU:0 before, /device:TPU:9 now
where the time goes in v1:
time: 191 us; the launch traced here: 190 us
  Pallas kernels  183 us (96%)
  local copies, waits for them, and re-layouts  6.57 us (3%)
    pallas_call x1, Pallas kernels, fused(): pl.pallas_call(kernel, out_shape=(jax.ShapeDtypeStruct(queries.shape, BF1...  183 us
    unnamed x8, local copies, waits for them, and re-layouts  6.57 us

profile of v1, /device:TPU:9, one launch (start us, length us, event | category | flops | bytes accessed | tf_op | source)
XLA Modules:
  0.0 190.3 jit_solution(261874421364021155)
XLA Ops:
  0.6 183.1 %shard_map.84 = (bf16[1,128,3072]{2,1,0:T(8,128)(2,1)}, bf16[1,128,3072]{2,1,0:T(8,128)(2,1)}, bf16[1,128,3072]{2,1,0:T(8,128)(2,1)}, f32[768,768]{1,0:T(8,128)}) custom-call(bf16[1,128,3072]{2,1,0:T(8,128)(2,1)} %q_ref.1, bf16[1,128,3072]{2,1,0:T(8,128)(2,1)} %k_ref.1, bf16[1,128,3072]{2,1,0:T(8,128)(2,1)} %v_ref.1, bf16[1,128,6144]{2,1,0:T(8,128)(2,1)} %go_ref.1, ...), custom_call_target="tpu_custom_call" | custom-call | flops 12079595520 | bytes 20971520 | tf_op jit(solution)/shard_map/pallas_call | solution.py:246
  183.7 0.0 copy-start.1
  183.7 0.0 copy-start
  183.7 2.2 %copy.13 = bf16[1,128,3072]{2,1,0:T(8,128)(2,1)} copy(bf16[1,128,3072]{2,1,0:T(8,128)(2,1)} %get-tuple-element.8) | data formatting | bytes 1572864
  186.0 2.1 %copy.14 = bf16[1,128,3072]{2,1,0:T(8,128)(2,1)} copy(bf16[1,128,3072]{2,1,0:T(8,128)(2,1)} %get-tuple-element.9) | data formatting | bytes 1572864
  188.0 0.0 copy-done.1
  188.0 0.9 copy.15
  188.9 0.0 copy-done
  188.9 1.4 copy.16
Async XLA Ops:
  183.7 4.3 %copy-start.1 = (bf16[1,128,3072]{2,1,0:T(8,128)(2,1)S(1)}, bf16[1,128,3072]{2,1,0:T(8,128)(2,1)}, u32[]{:S(2)}) copy-start(bf16[1,128,3072]{2,1,0:T(8,128)(2,1)} %get-tuple-element.10) | copy-start | bytes 2359300
  183.7 5.2 %copy-start = (f32[768,768]{1,0:T(8,128)S(1)}, f32[768,768]{1,0:T(8,128)}, u32[]{:S(2)}) copy-start(f32[768,768]{1,0:T(8,128)} %get-tuple-element.11) | copy-start | bytes 7077892

commit v2 on v1

--- a/solution.py
+++ b/solution.py
@@ -85,13 +85,22 @@
             got_g[r, c] = push(
                 go_ref.at[0, :, cols(owner, block)], g.at[r, rows(0), pl.ds(c * block, block)], row_peer[r]
             )
+    chunks = width // TILE
+    per = TILE // HEAD_DIM
+    got_qkv, own_qkv = {}, []
+    for c in range(chunks):
+        cc = pl.ds(c * TILE, TILE)
+        got_qkv[c] = []
+        for a, ref in enumerate((q_ref, k_ref, v_ref)):
+            for t in (2, 3, 1):
+                start = pl.multiple_of(tok_id[t] * width + c * TILE, 128)
+                got_qkv[c].append(
+                    push(ref.at[0, :, pl.ds(start, TILE)], qkv.at[a, rows(t), cc], tok_peer[t])
+                )
+    for a, ref in enumerate((q_ref, k_ref, v_ref)):
+        own_qkv.append(here(ref.at[0, :, cols(s, width)], qkv.at[a, rows(0)]))
     got_w = push(w_ref, w.at[:, pl.ds(block, block)], far)
     own_w = here(w_ref, w.at[:, pl.ds(0, block)])
-    got_qkv, own_qkv = [], []
-    for a, ref in enumerate((q_ref, k_ref, v_ref)):
-        for t in (2, 3, 1):
-            got_qkv.append(push(ref.at[0, :, cols(tok_id[t], width)], qkv.at[a, rows(t)], tok_peer[t]))
-        own_qkv.append(here(ref.at[0, :, cols(s, width)], qkv.at[a, rows(0)]))
 
     got_g2 = {}
 
@@ -99,18 +108,8 @@
         for t in (2, 1):
             got_g2[r, t] = push(g.at[r, rows(0)], g.at[r, rows(t)], tok_peer[t])
 
-    for copy in own:
+    for copy in own + own_qkv:
         copy.wait()
-    spread(0)
-    for r in (1, 2, 3):
-        got_g[r, 0].wait_recv()
-        got_g[r, 1].wait_recv()
-        spread(r)
-
-    for copy in own_qkv:
-        copy.wait()
-    for copy in got_qkv:
-        copy.wait_recv()
 
     def forward(h, carry):
         hc = cols(h, HEAD_DIM)
@@ -121,18 +120,35 @@
         att[0, :, hc] = jnp.dot(p.astype(BF16), qkv[2, :, hc], preferred_element_type=F32).astype(BF16)
         return carry
 
-    chunks = width // TILE
-    per = TILE // HEAD_DIM
+    order = (0, 3, 1, 2)
+    groups = [order[4 * c // chunks : 4 * (c + 1) // chunks] for c in range(chunks)]
     got_att = {}
     for c in range(chunks):
+        for copy in got_qkv[c]:
+            copy.wait_recv()
+        for r in groups[c]:
+            if r:
+                got_g[r, 0].wait_recv()
+                got_g[r, 1].wait_recv()
+            spread(r)
         lax.fori_loop(c * per, (c + 1) * per, forward, 0)
         cc = pl.ds(c * TILE, TILE)
         got_att[1, c] = push(att.at[0, :, cc], att.at[1, :, cc], row_peer[1])
         got_att[2, c] = push(att.at[0, :, cc], att.at[2, :, cc], row_peer[2])
 
-    for r in range(4):
+    def across_done(r):
         got_g2[r, 2].wait_recv()
         got_g2[r, 3] = push(g.at[r, rows(2)], g.at[r, rows(3)], tok_peer[1])
+
+    def relay(c):
+        got_att[2, c].wait_recv()
+        cc = pl.ds(c * TILE, TILE)
+        got_att[3, c] = push(att.at[2, :, cc], att.at[3, :, cc], row_peer[1])
+
+    for c in range(chunks - 1):
+        relay(c)
+    for r in order[:3]:
+        across_done(r)
     own_w.wait()
     got_w.wait_recv()
 
@@ -144,21 +160,19 @@
         got_g2[r, 3].wait_recv()
 
     got_p = {}
-    whole_rows(3)
-    whole_rows(1)
-    for c in range(chunks):
-        cc = pl.ds(c * TILE, TILE)
-        for slot, r in ((1, 3), (0, 1)):
+    for slot, r in ((1, 3), (0, 1)):
+        whole_rows(r)
+        for c in range(chunks):
+            cc = pl.ds(c * TILE, TILE)
             psend[slot, :, cc] = partial(r, c).astype(BF16)
             got_p[slot, c] = push(psend.at[slot, :, cc], pgot.at[slot, :, cc], row_peer[1])
-    whole_rows(2)
-    whole_rows(0)
-    for c in range(chunks):
-        cc = pl.ds(c * TILE, TILE)
-        keep[1, :, cc] = partial(2, c)
-        keep[0, :, cc] = partial(0, c)
-        got_att[2, c].wait_recv()
-        got_att[3, c] = push(att.at[2, :, cc], att.at[3, :, cc], row_peer[1])
+        if r == 3:
+            relay(chunks - 1)
+            across_done(2)
+    for slot, r in ((1, 2), (0, 0)):
+        whole_rows(r)
+        for c in range(chunks):
+            keep[slot, :, pl.ds(c * TILE, TILE)] = partial(r, c)
 
     for c in range(chunks):
         got_att[1, c].wait_recv()
@@ -268,8 +282,8 @@
             pltpu.VMEM((3, length, width), BF16),
             pltpu.VMEM((width, block), BF16),
             pltpu.VMEM((width, block), BF16),
-            pltpu.SemaphoreType.DMA((72,)),
-            pltpu.SemaphoreType.DMA((72,)),
+            pltpu.SemaphoreType.DMA((96,)),
+            pltpu.SemaphoreType.DMA((96,)),
             pltpu.SemaphoreType.DMA((16,)),
         ],
         compiler_params=pltpu.CompilerParams(

time: 191 us -> 160 us (0.84)
  Pallas kernels: 183 us -> 153 us
    pallas_call x1, Pallas kernels: 183 us -> 153 us  [fused(): pl.pallas_call(kernel, out_shape=(jax.ShapeDtypeStruct(queries.shape, BF1...]
where the time goes in v2:
time: 160 us
  Pallas kernels  153 us (96%)
  local copies, waits for them, and re-layouts  6.57 us (4%)
    pallas_call x1, Pallas kernels, fused(): pl.pallas_call(kernel, out_shape=(jax.ShapeDtypeStruct(queries.shape, BF1...  153 us
    unnamed x8, local copies, waits for them, and re-layouts  6.57 us

profile of v2, /device:TPU:9, one launch (start us, length us, event | category | flops | bytes accessed | tf_op | source)
XLA Modules:
  0.0 160.0 jit_solution(14270594359816109256)
XLA Ops:
  0.6 152.8 %shard_map.84 = (bf16[1,128,3072]{2,1,0:T(8,128)(2,1)}, bf16[1,128,3072]{2,1,0:T(8,128)(2,1)}, bf16[1,128,3072]{2,1,0:T(8,128)(2,1)}, f32[768,768]{1,0:T(8,128)}) custom-call(bf16[1,128,3072]{2,1,0:T(8,128)(2,1)} %q_ref.1, bf16[1,128,3072]{2,1,0:T(8,128)(2,1)} %k_ref.1, bf16[1,128,3072]{2,1,0:T(8,128)(2,1)} %v_ref.1, bf16[1,128,6144]{2,1,0:T(8,128)(2,1)} %go_ref.1, ...), custom_call_target="tpu_custom_call" | custom-call | flops 12079595520 | bytes 20971520 | tf_op jit(solution)/shard_map/pallas_call | solution.py:260
  153.5 0.0 copy-start.1
  153.5 0.0 copy-start
  153.5 2.2 %copy.13 = bf16[1,128,3072]{2,1,0:T(8,128)(2,1)} copy(bf16[1,128,3072]{2,1,0:T(8,128)(2,1)} %get-tuple-element.8) | data formatting | bytes 1572864
  155.7 2.1 %copy.14 = bf16[1,128,3072]{2,1,0:T(8,128)(2,1)} copy(bf16[1,128,3072]{2,1,0:T(8,128)(2,1)} %get-tuple-element.9) | data formatting | bytes 1572864
  157.7 0.0 copy-done.1
  157.8 0.9 copy.15
  158.6 0.0 copy-done
  158.6 1.4 copy.16
Async XLA Ops:
  153.5 4.3 %copy-start.1 = (bf16[1,128,3072]{2,1,0:T(8,128)(2,1)S(1)}, bf16[1,128,3072]{2,1,0:T(8,128)(2,1)}, u32[]{:S(2)}) copy-start(bf16[1,128,3072]{2,1,0:T(8,128)(2,1)} %get-tuple-element.10) | copy-start | bytes 2359300
  153.5 5.2 %copy-start = (f32[768,768]{1,0:T(8,128)S(1)}, f32[768,768]{1,0:T(8,128)}, u32[]{:S(2)}) copy-start(f32[768,768]{1,0:T(8,128)} %get-tuple-element.11) | copy-start | bytes 7077892

commit v3 on v2

--- a/solution.py
+++ b/solution.py
@@ -6,6 +6,7 @@
 from jax.sharding import PartitionSpec as P
 
 HEAD_DIM = 128
+LOG2_E = 1.4426950408889634
 TILE = 256
 MESH = pl.DeviceIdType.MESH
 F32, BF16 = jnp.float32, jnp.bfloat16
@@ -113,11 +114,14 @@
 
     def forward(h, carry):
         hc = cols(h, HEAD_DIM)
-        scores = lax.dot_general(qkv[0, :, hc], qkv[1, :, hc], NT, preferred_element_type=F32) * scale
-        expo = jnp.exp(scores - jnp.max(scores, axis=1, keepdims=True))
-        p = expo / jnp.sum(expo, axis=1, keepdims=True)
+        scores = lax.dot_general(qkv[1, :, hc], qkv[0, :, hc], NT, preferred_element_type=F32)
+        top = jnp.max(scores, axis=0, keepdims=True) * (scale * LOG2_E)
+        expo = jnp.exp2(scores * (scale * LOG2_E) - top)
+        p = expo * (1.0 / jnp.sum(expo, axis=0, keepdims=True))
         probs[h] = p
-        att[0, :, hc] = jnp.dot(p.astype(BF16), qkv[2, :, hc], preferred_element_type=F32).astype(BF16)
+        att[0, hc, :] = lax.dot_general(
+            qkv[2, :, hc], p.astype(BF16), TN, preferred_element_type=F32
+        ).astype(BF16)
         return carry
 
     order = (0, 3, 1, 2)
@@ -133,8 +137,8 @@
             spread(r)
         lax.fori_loop(c * per, (c + 1) * per, forward, 0)
         cc = pl.ds(c * TILE, TILE)
-        got_att[1, c] = push(att.at[0, :, cc], att.at[1, :, cc], row_peer[1])
-        got_att[2, c] = push(att.at[0, :, cc], att.at[2, :, cc], row_peer[2])
+        got_att[1, c] = push(att.at[0, cc], att.at[1, cc], row_peer[1])
+        got_att[2, c] = push(att.at[0, cc], att.at[2, cc], row_peer[2])
 
     def across_done(r):
         got_g2[r, 2].wait_recv()
@@ -143,7 +147,7 @@
     def relay(c):
         got_att[2, c].wait_recv()
         cc = pl.ds(c * TILE, TILE)
-        got_att[3, c] = push(att.at[2, :, cc], att.at[3, :, cc], row_peer[1])
+        got_att[3, c] = push(att.at[2, cc], att.at[3, cc], row_peer[1])
 
     for c in range(chunks - 1):
         relay(c)
@@ -181,7 +185,7 @@
     def weight_tile(start):
         total = jnp.zeros((width, TILE), F32)
         for r in range(4):
-            total += lax.dot_general(att[r], g[r, :, pl.ds(start, TILE)], TN, preferred_element_type=F32)
+            total += jnp.dot(att[r], g[r, :, pl.ds(start, TILE)], preferred_element_type=F32)
         return total
 
     got_gw = []
@@ -217,12 +221,13 @@
         hc = cols(h, HEAD_DIM)
         q, k, v, do = qkv[0, :, hc], qkv[1, :, hc], qkv[2, :, hc], dout[:, hc]
         p = probs[h]
-        delta = jnp.sum(do.astype(F32) * att[0, :, hc].astype(F32), axis=1, keepdims=True)
-        grad_p = lax.dot_general(do, v, NT, preferred_element_type=F32)
+        delta = jnp.sum(do.astype(F32).T * att[0, hc, :].astype(F32), axis=0, keepdims=True)
+        grad_p = lax.dot_general(v, do, NT, preferred_element_type=F32)
         grad_s = (p * (grad_p - delta)).astype(BF16)
-        grads[0, :, hc] = (jnp.dot(grad_s, k, preferred_element_type=F32) * scale).astype(BF16)
-        grads[1, :, hc] = (lax.dot_general(grad_s, q, TN, preferred_element_type=F32) * scale).astype(BF16)
-        grads[2, :, hc] = lax.dot_general(p.astype(BF16), do, TN, preferred_element_type=F32).astype(BF16)
+        grad_q = lax.dot_general(k, grad_s, TN, preferred_element_type=F32) * scale
+        grads[0, :, hc] = grad_q.T.astype(BF16)
+        grads[1, :, hc] = (jnp.dot(grad_s, q, preferred_element_type=F32) * scale).astype(BF16)
+        grads[2, :, hc] = jnp.dot(p.astype(BF16), do, preferred_element_type=F32).astype(BF16)
         for a in range(3):
             for t in (2, 3, 1):
                 home(a, t, hc, s * width + h * HEAD_DIM, HEAD_DIM).start()
@@ -257,7 +262,7 @@
     heads = width // HEAD_DIM
     any_spec = pl.BlockSpec(memory_space=pl.ANY)
     flops = 4 * length * width * grad_out.shape[2] + 12 * heads * length * length * HEAD_DIM
-    return pl.pallas_call(
+    results = pl.pallas_call(
         kernel,
         out_shape=(
             jax.ShapeDtypeStruct(queries.shape, BF16),
@@ -271,7 +276,7 @@
             pltpu.VMEM((3, length, width), BF16),
             pltpu.VMEM((4, length, 2 * block), BF16),
             pltpu.VMEM((width, 2 * block), BF16),
-            pltpu.VMEM((4, length, width), BF16),
+            pltpu.VMEM((4, width, length), BF16),
             pltpu.VMEM((heads, length, length), F32),
             pltpu.VMEM((2, length, width), F32),
             pltpu.VMEM((2, length, width), BF16),
@@ -291,6 +296,26 @@
         ),
         cost_estimate=pl.CostEstimate(flops=flops, bytes_accessed=20 * 1024 * 1024, transcendentals=0),
     )(queries, attn_keys, attn_values, grad_out, out_weight)
+    return place(*results)
+
+
+def place_kernel(*refs):
+    for src, dst in zip(refs[:4], refs[4:]):
+        dst[...] = src[...]
+
+
+def place(*results):
+    steps = 4
+    specs = [pl.BlockSpec((1, x.shape[1] // steps, x.shape[2]), lambda i: (0, i, 0)) for x in results[:3]]
+    specs.append(pl.BlockSpec((results[3].shape[0] // steps, results[3].shape[1]), lambda i: (i, 0)))
+    return pl.pallas_call(
+        place_kernel,
+        grid=(steps,),
+        out_shape=tuple(jax.ShapeDtypeStruct(x.shape, x.dtype) for x in results),
+        in_specs=specs,
+        out_specs=tuple(specs),
+        compiler_params=pltpu.CompilerParams(vmem_limit_bytes=60 * 1024 * 1024),
+    )(*results)
 
 
 def head_pass(q, k, v, dout):
@@ -338,7 +363,7 @@
 def shards(queries, attn_keys, attn_values, grad_out, out_weight):
     width, block = out_weight.shape
     fits = lax.axis_size("seq") == 4 and lax.axis_size("fsdp") == 8
-    if fits and queries.shape[0] == 1 and queries.shape[1] % 16 == 0 and width % TILE == 0 and block % TILE == 0:
+    if fits and queries.shape[0] == 1 and queries.shape[1] % 64 == 0 and width % TILE == 0 and block % TILE == 0:
         return fused(queries, attn_keys, attn_values, grad_out, out_weight)
     return collectives(queries, attn_keys, attn_values, grad_out, out_weight)
 

time: 160 us -> 159 us (level)
  local copies, waits for them, and re-layouts: 6.57 us -> 0 us
  Pallas kernels: 153 us -> 158 us
    unnamed x8 -> x0, local copies, waits for them, and re-layouts: 6.57 us -> none
    pallas_call x0 -> x1, Pallas kernels: none -> 5.1 us  [place(): pl.pallas_call(place_kernel, grid=(steps,), out_shape=tuple((jax.ShapeDty...]
where the time goes in v3:
time: 159 us; the launch traced here: 158 us
  Pallas kernels  158 us (99%)
    pallas_call x1, Pallas kernels, fused(): pl.pallas_call(kernel, out_shape=(jax.ShapeDtypeStruct(queries.shape, BF1...  153 us
    pallas_call x1, Pallas kernels, place(): pl.pallas_call(place_kernel, grid=(steps,), out_shape=tuple((jax.ShapeDty...  5.1 us

profile of v3, /device:TPU:9, one launch (start us, length us, event | category | flops | bytes accessed | tf_op | source)
XLA Modules:
  0.0 158.3 jit_solution(15566741482497138776)
XLA Ops:
  0.6 152.6 %shard_map.84 = (bf16[1,128,3072]{2,1,0:T(8,128)(2,1)}, bf16[1,128,3072]{2,1,0:T(8,128)(2,1)}, bf16[1,128,3072]{2,1,0:T(8,128)(2,1)}, f32[768,768]{1,0:T(8,128)}) custom-call(bf16[1,128,3072]{2,1,0:T(8,128)(2,1)} %q_ref.1, bf16[1,128,3072]{2,1,0:T(8,128)(2,1)} %k_ref.1, bf16[1,128,3072]{2,1,0:T(8,128)(2,1)} %v_ref.1, bf16[1,128,6144]{2,1,0:T(8,128)(2,1)} %go_ref.1, ...), custom_call_target="tpu_custom_call" | custom-call | flops 12079595520 | bytes 20971520 | tf_op jit(solution)/shard_map/pallas_call | solution.py:265
  153.2 5.1 %shard_map.85 = (bf16[1,128,3072]{2,1,0:T(8,128)(2,1)}, bf16[1,128,3072]{2,1,0:T(8,128)(2,1)}, bf16[1,128,3072]{2,1,0:T(8,128)(2,1)}, f32[768,768]{1,0:T(8,128)}) custom-call(bf16[1,128,3072]{2,1,0:T(8,128)(2,1)} %get-tuple-element.8.refs_0_, bf16[1,128,3072]{2,1,0:T(8,128)(2,1)} %get-tuple-element.9.refs_1_, ...), custom_call_target="tpu_custom_call" | custom-call | tf_op jit(solution)/shard_map/pallas_call | solution.py:311

commit v4 on v3

--- a/solution.py
+++ b/solution.py
@@ -30,11 +30,11 @@
     across = s + 2 - 4 * (s // 2)
     both = core + 2 - 4 * (core // 2)
     f_y = f + 1 - 2 * (f % 2)
-    f_z = f + 2 - 4 * ((f // 2) % 2)
+    f_z = f + 4 - 8 * (f // 4)
     f_yz = f_z + 1 - 2 * (f_z % 2)
 
     def other_half(i):
-        return i + 4 - 8 * (i // 4)
+        return i + 2 - 4 * ((i // 2) % 2)
 
     tok_peer = [None] + [{"seq": i, "fsdp": f} for i in (core, across, both)]
     tok_id = [s, core, across, both]
@@ -89,7 +89,8 @@
     chunks = width // TILE
     per = TILE // HEAD_DIM
     got_qkv, own_qkv = {}, []
-    for c in range(chunks):
+
+    def send_qkv(c):
         cc = pl.ds(c * TILE, TILE)
         got_qkv[c] = []
         for a, ref in enumerate((q_ref, k_ref, v_ref)):
@@ -98,6 +99,8 @@
                 got_qkv[c].append(
                     push(ref.at[0, :, pl.ds(start, TILE)], qkv.at[a, rows(t), cc], tok_peer[t])
                 )
+
+    send_qkv(0)
     for a, ref in enumerate((q_ref, k_ref, v_ref)):
         own_qkv.append(here(ref.at[0, :, cols(s, width)], qkv.at[a, rows(0)]))
     got_w = push(w_ref, w.at[:, pl.ds(block, block)], far)
@@ -111,6 +114,14 @@
 
     for copy in own + own_qkv:
         copy.wait()
+    order = (0, 3, 1, 2)
+    for r in order:
+        if r:
+            got_g[r, 0].wait_recv()
+            got_g[r, 1].wait_recv()
+        spread(r)
+    for c in range(1, chunks):
+        send_qkv(c)
 
     def forward(h, carry):
         hc = cols(h, HEAD_DIM)
@@ -124,21 +135,17 @@
         ).astype(BF16)
         return carry
 
-    order = (0, 3, 1, 2)
-    groups = [order[4 * c // chunks : 4 * (c + 1) // chunks] for c in range(chunks)]
     got_att = {}
-    for c in range(chunks):
+
+    def attend(c):
         for copy in got_qkv[c]:
             copy.wait_recv()
-        for r in groups[c]:
-            if r:
-                got_g[r, 0].wait_recv()
-                got_g[r, 1].wait_recv()
-            spread(r)
         lax.fori_loop(c * per, (c + 1) * per, forward, 0)
         cc = pl.ds(c * TILE, TILE)
         got_att[1, c] = push(att.at[0, cc], att.at[1, cc], row_peer[1])
         got_att[2, c] = push(att.at[0, cc], att.at[2, cc], row_peer[2])
+
+    attend(0)
 
     def across_done(r):
         got_g2[r, 2].wait_recv()
@@ -149,10 +156,9 @@
         cc = pl.ds(c * TILE, TILE)
         got_att[3, c] = push(att.at[2, cc], att.at[3, cc], row_peer[1])
 
-    for c in range(chunks - 1):
-        relay(c)
     for r in order[:3]:
         across_done(r)
+    relay(0)
     own_w.wait()
     got_w.wait_recv()
 
@@ -171,28 +177,16 @@
             psend[slot, :, cc] = partial(r, c).astype(BF16)
             got_p[slot, c] = push(psend.at[slot, :, cc], pgot.at[slot, :, cc], row_peer[1])
         if r == 3:
-            relay(chunks - 1)
             across_done(2)
     for slot, r in ((1, 2), (0, 0)):
         whole_rows(r)
         for c in range(chunks):
             keep[slot, :, pl.ds(c * TILE, TILE)] = partial(r, c)
 
-    for c in range(chunks):
-        got_att[1, c].wait_recv()
-        got_att[3, c].wait_recv()
-
-    def weight_tile(start):
-        total = jnp.zeros((width, TILE), F32)
-        for r in range(4):
-            total += jnp.dot(att[r], g[r, :, pl.ds(start, TILE)], preferred_element_type=F32)
-        return total
-
-    got_gw = []
-    for c in range(block // TILE):
-        cc = pl.ds(c * TILE, TILE)
-        gwsend[:, cc] = weight_tile(block + c * TILE).astype(BF16)
-        got_gw.append(push(gwsend.at[:, cc], gwgot.at[:, cc], far))
+    for c in range(1, chunks):
+        attend(c)
+    for c in range(1, chunks):
+        relay(c)
 
     got_z = []
     for c in range(chunks):
@@ -200,9 +194,6 @@
         got_p[1, c].wait_recv()
         zsend[:, cc] = (keep[1, :, cc] + pgot[1, :, cc].astype(F32)).astype(BF16)
         got_z.append(push(zsend.at[:, cc], zgot.at[:, cc], row_peer[2]))
-
-    for c in range(block // TILE):
-        gw_out[:, pl.ds(c * TILE, TILE)] = weight_tile(c * TILE)
 
     outs = (gq_out, gk_out, gv_out)
     base = count[0]
@@ -233,12 +224,33 @@
                 home(a, t, hc, s * width + h * HEAD_DIM, HEAD_DIM).start()
         return carry
 
-    for c in range(chunks):
+    def differentiate(c):
         cc = pl.ds(c * TILE, TILE)
         got_p[0, c].wait_recv()
         got_z[c].wait_recv()
         dout[:, cc] = (keep[0, :, cc] + pgot[0, :, cc].astype(F32) + zgot[:, cc].astype(F32)).astype(BF16)
         lax.fori_loop(c * per, (c + 1) * per, backward, 0)
+
+    for c in range(chunks - 1):
+        differentiate(c)
+
+    def weight_tile(start):
+        total = jnp.zeros((width, TILE), F32)
+        for r in range(4):
+            total += jnp.dot(att[r], g[r, :, pl.ds(start, TILE)], preferred_element_type=F32)
+        return total
+
+    for c in range(chunks):
+        got_att[1, c].wait_recv()
+        got_att[3, c].wait_recv()
+    got_gw = []
+    for c in range(block // TILE):
+        cc = pl.ds(c * TILE, TILE)
+        gwsend[:, cc] = weight_tile(block + c * TILE).astype(BF16)
+        got_gw.append(push(gwsend.at[:, cc], gwgot.at[:, cc], far))
+    differentiate(chunks - 1)
+    for c in range(block // TILE):
+        gw_out[:, pl.ds(c * TILE, TILE)] = weight_tile(c * TILE)
 
     last = [here(grads.at[a, rows(0)], outs[a].at[0, :, cols(s, width)]) for a in range(3)]
     for copy in got_gw:

time: 159 us -> 159 us (level)
  the two profiles are of different devices: /device:TPU:9 before, /device:TPU:0 now
where the time goes in v4:
time: 159 us; the launch traced here: 158 us
  Pallas kernels  158 us (99%)
    pallas_call x1, Pallas kernels, fused(): pl.pallas_call(kernel, out_shape=(jax.ShapeDtypeStruct(queries.shape, BF1...  153 us
    pallas_call x1, Pallas kernels, place(): pl.pallas_call(place_kernel, grid=(steps,), out_shape=tuple((jax.ShapeDty...  5.1 us

profile of v4, /device:TPU:0, one launch (start us, length us, event | category | flops | bytes accessed | tf_op | source)
XLA Modules:
  0.0 158.4 jit_solution(14883494810396788023)
XLA Ops:
  0.6 152.6 %shard_map.84 = (bf16[1,128,3072]{2,1,0:T(8,128)(2,1)}, bf16[1,128,3072]{2,1,0:T(8,128)(2,1)}, bf16[1,128,3072]{2,1,0:T(8,128)(2,1)}, f32[768,768]{1,0:T(8,128)}) custom-call(bf16[1,128,3072]{2,1,0:T(8,128)(2,1)} %q_ref.1, bf16[1,128,3072]{2,1,0:T(8,128)(2,1)} %k_ref.1, bf16[1,128,3072]{2,1,0:T(8,128)(2,1)} %v_ref.1, bf16[1,128,6144]{2,1,0:T(8,128)(2,1)} %go_ref.1, ...), custom_call_target="tpu_custom_call" | custom-call | flops 12079595520 | bytes 20971520 | tf_op jit(solution)/shard_map/pallas_call | solution.py:277
  153.3 5.1 %shard_map.85 = (bf16[1,128,3072]{2,1,0:T(8,128)(2,1)}, bf16[1,128,3072]{2,1,0:T(8,128)(2,1)}, bf16[1,128,3072]{2,1,0:T(8,128)(2,1)}, f32[768,768]{1,0:T(8,128)}) custom-call(bf16[1,128,3072]{2,1,0:T(8,128)(2,1)} %get-tuple-element.8.refs_0_, bf16[1,128,3072]{2,1,0:T(8,128)(2,1)} %get-tuple-element.9.refs_1_, ...), custom_call_target="tpu_custom_call" | custom-call | tf_op jit(solution)/shard_map/pallas_call | solution.py:323

commit v5 on v3

--- a/solution.py
+++ b/solution.py
@@ -30,11 +30,11 @@
     across = s + 2 - 4 * (s // 2)
     both = core + 2 - 4 * (core // 2)
     f_y = f + 1 - 2 * (f % 2)
-    f_z = f + 2 - 4 * ((f // 2) % 2)
+    f_z = f + 4 - 8 * (f // 4)
     f_yz = f_z + 1 - 2 * (f_z % 2)
 
     def other_half(i):
-        return i + 4 - 8 * (i // 4)
+        return i + 2 - 4 * ((i // 2) % 2)
 
     tok_peer = [None] + [{"seq": i, "fsdp": f} for i in (core, across, both)]
     tok_id = [s, core, across, both]
@@ -80,7 +80,7 @@
         owner = f if c == 0 else other_half(f)
         own.append(here(go_ref.at[0, :, cols(owner, block)], g.at[0, rows(0), pl.ds(c * block, block)]))
     got_g = {}
-    for r in (3, 1, 2):
+    for r in (1, 3, 2):
         for c in range(2):
             owner = row_id[r] if c == 0 else other_half(row_id[r])
             got_g[r, c] = push(
@@ -89,7 +89,8 @@
     chunks = width // TILE
     per = TILE // HEAD_DIM
     got_qkv, own_qkv = {}, []
-    for c in range(chunks):
+
+    def send_qkv(c):
         cc = pl.ds(c * TILE, TILE)
         got_qkv[c] = []
         for a, ref in enumerate((q_ref, k_ref, v_ref)):
@@ -98,6 +99,8 @@
                 got_qkv[c].append(
                     push(ref.at[0, :, pl.ds(start, TILE)], qkv.at[a, rows(t), cc], tok_peer[t])
                 )
+
+    send_qkv(0)
     for a, ref in enumerate((q_ref, k_ref, v_ref)):
         own_qkv.append(here(ref.at[0, :, cols(s, width)], qkv.at[a, rows(0)]))
     got_w = push(w_ref, w.at[:, pl.ds(block, block)], far)
@@ -111,6 +114,16 @@
 
     for copy in own + own_qkv:
         copy.wait()
+
+    def arrived(r):
+        got_g[r, 0].wait_recv()
+        got_g[r, 1].wait_recv()
+        spread(r)
+
+    spread(0)
+    arrived(1)
+    for c in range(1, chunks):
+        send_qkv(c)
 
     def forward(h, carry):
         hc = cols(h, HEAD_DIM)
@@ -124,21 +137,21 @@
         ).astype(BF16)
         return carry
 
-    order = (0, 3, 1, 2)
-    groups = [order[4 * c // chunks : 4 * (c + 1) // chunks] for c in range(chunks)]
     got_att = {}
-    for c in range(chunks):
+
+    def attend(c):
         for copy in got_qkv[c]:
             copy.wait_recv()
-        for r in groups[c]:
-            if r:
-                got_g[r, 0].wait_recv()
-                got_g[r, 1].wait_recv()
-            spread(r)
         lax.fori_loop(c * per, (c + 1) * per, forward, 0)
         cc = pl.ds(c * TILE, TILE)
         got_att[1, c] = push(att.at[0, cc], att.at[1, cc], row_peer[1])
         got_att[2, c] = push(att.at[0, cc], att.at[2, cc], row_peer[2])
+
+    for c in range(chunks - 1):
+        attend(c)
+    arrived(3)
+    arrived(2)
+    attend(chunks - 1)
 
     def across_done(r):
         got_g2[r, 2].wait_recv()
@@ -151,8 +164,8 @@
 
     for c in range(chunks - 1):
         relay(c)
-    for r in order[:3]:
-        across_done(r)
+    across_done(0)
+    across_done(1)
     own_w.wait()
     got_w.wait_recv()
 
@@ -164,23 +177,26 @@
         got_g2[r, 3].wait_recv()
 
     got_p = {}
-    for slot, r in ((1, 3), (0, 1)):
+
+    def send_partial(slot, r):
         whole_rows(r)
         for c in range(chunks):
             cc = pl.ds(c * TILE, TILE)
             psend[slot, :, cc] = partial(r, c).astype(BF16)
             got_p[slot, c] = push(psend.at[slot, :, cc], pgot.at[slot, :, cc], row_peer[1])
-        if r == 3:
-            relay(chunks - 1)
-            across_done(2)
-    for slot, r in ((1, 2), (0, 0)):
+
+    def keep_partial(slot, r):
         whole_rows(r)
         for c in range(chunks):
             keep[slot, :, pl.ds(c * TILE, TILE)] = partial(r, c)
 
-    for c in range(chunks):
-        got_att[1, c].wait_recv()
-        got_att[3, c].wait_recv()
+    send_partial(0, 1)
+    relay(chunks - 1)
+    keep_partial(0, 0)
+    across_done(3)
+    across_done(2)
+    send_partial(1, 3)
+    keep_partial(1, 2)
 
     def weight_tile(start):
         total = jnp.zeros((width, TILE), F32)
@@ -188,6 +204,9 @@
             total += jnp.dot(att[r], g[r, :, pl.ds(start, TILE)], preferred_element_type=F32)
         return total
 
+    for c in range(chunks):
+        got_att[1, c].wait_recv()
+        got_att[3, c].wait_recv()
     got_gw = []
     for c in range(block // TILE):
         cc = pl.ds(c * TILE, TILE)
@@ -233,12 +252,15 @@
                 home(a, t, hc, s * width + h * HEAD_DIM, HEAD_DIM).start()
         return carry
 
-    for c in range(chunks):
+    def differentiate(c):
         cc = pl.ds(c * TILE, TILE)
         got_p[0, c].wait_recv()
         got_z[c].wait_recv()
         dout[:, cc] = (keep[0, :, cc] + pgot[0, :, cc].astype(F32) + zgot[:, cc].astype(F32)).astype(BF16)
         lax.fori_loop(c * per, (c + 1) * per, backward, 0)
+
+    for c in range(chunks):
+        differentiate(c)
 
     last = [here(grads.at[a, rows(0)], outs[a].at[0, :, cols(s, width)]) for a in range(3)]
     for copy in got_gw:

time: 159 us -> 168 us (1.057)
  Pallas kernels: 158 us -> 167 us
    pallas_call x1, Pallas kernels: 153 us -> 162 us  [fused(): pl.pallas_call(kernel, out_shape=(jax.ShapeDtypeStruct(queries.shape, BF1...]
where the time goes in v5:
time: 168 us
  Pallas kernels  167 us (99%)
    pallas_call x1, Pallas kernels, fused(): pl.pallas_call(kernel, out_shape=(jax.ShapeDtypeStruct(queries.shape, BF1...  162 us
    pallas_call x1, Pallas kernels, place(): pl.pallas_call(place_kernel, grid=(steps,), out_shape=tuple((jax.ShapeDty...  5.1 us

profile of v5, /device:TPU:9, one launch (start us, length us, event | category | flops | bytes accessed | tf_op | source)
XLA Modules:
  0.0 167.9 jit_solution(13338307488650494214)
XLA Ops:
  0.6 162.2 %shard_map.84 = (bf16[1,128,3072]{2,1,0:T(8,128)(2,1)}, bf16[1,128,3072]{2,1,0:T(8,128)(2,1)}, bf16[1,128,3072]{2,1,0:T(8,128)(2,1)}, f32[768,768]{1,0:T(8,128)}) custom-call(bf16[1,128,3072]{2,1,0:T(8,128)(2,1)} %q_ref.1, bf16[1,128,3072]{2,1,0:T(8,128)(2,1)} %k_ref.1, bf16[1,128,3072]{2,1,0:T(8,128)(2,1)} %v_ref.1, bf16[1,128,6144]{2,1,0:T(8,128)(2,1)} %go_ref.1, ...), custom_call_target="tpu_custom_call" | custom-call | flops 12079595520 | bytes 20971520 | tf_op jit(solution)/shard_map/pallas_call | solution.py:287
  162.8 5.1 %shard_map.85 = (bf16[1,128,3072]{2,1,0:T(8,128)(2,1)}, bf16[1,128,3072]{2,1,0:T(8,128)(2,1)}, bf16[1,128,3072]{2,1,0:T(8,128)(2,1)}, f32[768,768]{1,0:T(8,128)}) custom-call(bf16[1,128,3072]{2,1,0:T(8,128)(2,1)} %get-tuple-element.8.refs_0_, bf16[1,128,3072]{2,1,0:T(8,128)(2,1)} %get-tuple-element.9.refs_1_, ...), custom_call_target="tpu_custom_call" | custom-call | tf_op jit(solution)/shard_map/pallas_call | solution.py:333

commit v6 on v3

--- a/solution.py
+++ b/solution.py
@@ -173,11 +173,8 @@
         if r == 3:
             relay(chunks - 1)
             across_done(2)
-    for slot, r in ((1, 2), (0, 0)):
-        whole_rows(r)
-        for c in range(chunks):
-            keep[slot, :, pl.ds(c * TILE, TILE)] = partial(r, c)
-
+    whole_rows(2)
+    whole_rows(0)
     for c in range(chunks):
         got_att[1, c].wait_recv()
         got_att[3, c].wait_recv()
@@ -193,6 +190,10 @@
         cc = pl.ds(c * TILE, TILE)
         gwsend[:, cc] = weight_tile(block + c * TILE).astype(BF16)
         got_gw.append(push(gwsend.at[:, cc], gwgot.at[:, cc], far))
+
+    for slot, r in ((1, 2), (0, 0)):
+        for c in range(chunks):
+            keep[slot, :, pl.ds(c * TILE, TILE)] = partial(r, c)
 
     got_z = []
     for c in range(chunks):

time: 159 us -> 158 us (level)
  no operation moved by 1% of the time
where the time goes in v6:
time: 158 us
  Pallas kernels  157 us (99%)
    pallas_call x1, Pallas kernels, fused(): pl.pallas_call(kernel, out_shape=(jax.ShapeDtypeStruct(queries.shape, BF1...  152 us
    pallas_call x1, Pallas kernels, place(): pl.pallas_call(place_kernel, grid=(steps,), out_shape=tuple((jax.ShapeDty...  5.1 us

profile of v6, /device:TPU:9, one launch (start us, length us, event | category | flops | bytes accessed | tf_op | source)
XLA Modules:
  0.0 157.5 jit_solution(16004542107690383011)
XLA Ops:
  0.6 151.8 %shard_map.84 = (bf16[1,128,3072]{2,1,0:T(8,128)(2,1)}, bf16[1,128,3072]{2,1,0:T(8,128)(2,1)}, bf16[1,128,3072]{2,1,0:T(8,128)(2,1)}, f32[768,768]{1,0:T(8,128)}) custom-call(bf16[1,128,3072]{2,1,0:T(8,128)(2,1)} %q_ref.1, bf16[1,128,3072]{2,1,0:T(8,128)(2,1)} %k_ref.1, bf16[1,128,3072]{2,1,0:T(8,128)(2,1)} %v_ref.1, bf16[1,128,6144]{2,1,0:T(8,128)(2,1)} %go_ref.1, ...), custom_call_target="tpu_custom_call" | custom-call | flops 12079595520 | bytes 20971520 | tf_op jit(solution)/shard_map/pallas_call | solution.py:266
  152.4 5.1 %shard_map.85 = (bf16[1,128,3072]{2,1,0:T(8,128)(2,1)}, bf16[1,128,3072]{2,1,0:T(8,128)(2,1)}, bf16[1,128,3072]{2,1,0:T(8,128)(2,1)}, f32[768,768]{1,0:T(8,128)}) custom-call(bf16[1,128,3072]{2,1,0:T(8,128)(2,1)} %get-tuple-element.8.refs_0_, bf16[1,128,3072]{2,1,0:T(8,128)(2,1)} %get-tuple-element.9.refs_1_, ...), custom_call_target="tpu_custom_call" | custom-call | tf_op jit(solution)/shard_map/pallas_call | solution.py:312
